TPU v7x, 32 devices: a whole 2x2x4 slice. The times are simulated.
32 devices in a mesh: row: 4 (over y, core), col: 8 (over z, x).
Axes of the slice: x: 2, y: 2, z: 4, core: 2. Of those that a mesh axis runs over, the one named last changes fastest.
Arguments:
- query_grads: bfloat16 [256, 8192], P('row', 'col'), may hold values from -6 to 6
- query_acts: bfloat16 [256, 8192], P('col', 'row'), may hold values from -6 to 6
- train_grads: bfloat16 [512, 8192], P('row', 'col'), may hold values from -6 to 6
- train_acts: bfloat16 [512, 8192], P('col', 'row'), may hold values from -6 to 6
- grad_basis: bfloat16 [8192, 8192], P('col', 'row'), may hold values from -0.0625 to 0.0625
- act_basis: bfloat16 [8192, 8192], P('row', 'col'), may hold values from -0.0625 to 0.0625
- eigen_corr: float32 [8192, 8192], P('row', 'col'), may hold values from 0.02 to 2
- damping: float32 [], replicated, may hold values from 0.05 to 0.5
- query_seq: int32 [256], replicated, may hold values from 0 to 31, never falling along the last dimension, each value on 1 to 16 neighbouring positions
- train_doc: int32 [512], replicated, may hold values from 0 to 15, never falling along the last dimension, each value on 1 to 64 neighbouring positions
Outputs:
- scores: float32 [32, 512], P(None, 'col')
- doc_scores: float32 [32, 16], replicated
Inputs may be any that keep to these rules, and one draw needn't show every extreme that they name: `query_seq`: Non-decreasing along the query tokens; every sequence has 1 to 16 tokens, and one has exactly that many. `train_doc`: Non-decreasing along the training tokens; every document has 1 to 64 tokens, and one has exactly that many.
All inputs are finite; a program needn't handle non-finite values.
Results may differ from a plain program's by a relative error of at most 0.005.
Values may be sent and summed in bfloat16 or wider, within the bound.
A program may use at most 64 MiB of HBM per device.

v0:
```python
import jax
import jax.numpy as jnp
from jax import lax
from jax.sharding import PartitionSpec as P

D = 8192
S = 32
DOCS = 16


def local(
    query_grads,
    query_acts,
    train_grads,
    train_acts,
    grad_basis,
    act_basis,
    eigen_corr,
    damping,
    query_seq,
    train_doc,
):
    grad_query, grad_train = (
        lax.all_gather(query_grads, "row", axis=0, tiled=True),
        lax.all_gather(train_grads, "row", axis=0, tiled=True),
    )
    act_query, act_train = (
        lax.all_gather(query_acts, "col", axis=0, tiled=True),
        lax.all_gather(train_acts, "col", axis=0, tiled=True),
    )
    grads_all = jnp.concatenate([grad_query, grad_train], axis=0)
    acts_all = jnp.concatenate([act_query, act_train], axis=0)
    n_query = grad_query.shape[0]
    grad_part = jnp.dot(grads_all, grad_basis, preferred_element_type=jnp.float32)
    grads_rot = lax.psum(grad_part, "col").astype(jnp.bfloat16)
    act_part = jnp.dot(acts_all, act_basis, preferred_element_type=jnp.float32)
    acts_rot = lax.psum(act_part, "row").astype(jnp.bfloat16)
    rot_gq = grads_rot[:n_query]
    rot_gu = grads_rot[n_query:]
    rot_aq = acts_rot[:n_query]
    rot_au = acts_rot[n_query:]
    denom = eigen_corr + damping
    act_wide = rot_au.astype(jnp.float32)
    row_block = eigen_corr.shape[0]
    col_block = eigen_corr.shape[1]
    group = 4

    def score_group(first):
        seq_ids = first + jnp.arange(group, dtype=jnp.int32)
        member = (query_seq[:, None] == seq_ids[None, :]).astype(jnp.bfloat16)
        weighted = (member[:, :, None] * rot_gq[:, None, :]).reshape(n_query, group * row_block)
        outer = lax.dot_general(
            weighted, rot_aq, (((0,), (0,)), ((), ())), preferred_element_type=jnp.float32
        )
        precond = (outer.reshape(group, row_block, col_block) / denom[None, :, :]).astype(
            jnp.bfloat16
        )
        mapped = jnp.einsum("ui,sij->usj", rot_gu, precond, preferred_element_type=jnp.float32)
        return jnp.sum(mapped * act_wide[:, None, :], axis=2).T

    starts = jnp.arange(S // group, dtype=jnp.int32) * group
    partial_scores = lax.map(score_group, starts).reshape(S, rot_gu.shape[0]) / D
    doc_table = (train_doc[:, None] == jnp.arange(DOCS, dtype=jnp.int32)[None, :]).astype(
        jnp.float32
    )
    counts = jnp.sum(doc_table, axis=0)
    owned = rot_gu.shape[0] // lax.axis_size("col")
    first_owned = lax.axis_index("col") * owned
    share = lax.psum_scatter(partial_scores, "col", scatter_dimension=1, tiled=True)
    scores = lax.psum(share, "row")
    owned_docs = lax.dynamic_slice_in_dim(doc_table, first_owned, owned, 0)
    doc_part = jnp.dot(scores, owned_docs, precision=lax.Precision.HIGHEST)
    doc_sum = lax.psum(doc_part, "col")
    return (scores, doc_sum / counts[None, :])


def solution(mesh):
    in_specs = (
        P("row", "col"),
        P("col", "row"),
        P("row", "col"),
        P("col", "row"),
        P("col", "row"),
        P("row", "col"),
        P("row", "col"),
        P(),
        P(),
        P(),
    )
    out_specs = (P(None, "col"), P())
    return jax.shard_map(local, mesh=mesh, in_specs=in_specs, out_specs=out_specs, check_vma=False)
```

profile of v0, /device:TPU:11, one launch (start us, length us, event | category | flops | bytes accessed | tf_op | source)
XLA Modules:
  0.0 611.6 jit_solution(4301126775290471905)
XLA Ops:
  7.2 0.7 all-gather.4.cloned.1.call-update
  7.9 0.7 all-gather.6.cloned.1.call-update
  8.7 0.7 all-gather.8.cloned.1.call-update
  9.4 7.9 %all_gather.12 = bf16[256,1024]{1,0:T(8,128)(2,1)S(1)} all-gather(bf16[64,1024]{1,0:T(8,128)(2,1)} %param.12), channel_id=1, replica_groups=mesh['row'=4,'col'=8] {'row'}, dimensions={0}, use_global_device_ids=true | all-gather | bytes 655360 | tf_op jit(solution)/shard_map/all_gather | solution.py:24
  18.0 8.7 %broadcast_add_fusion = f32[2048,1024]{1,0:T(8,128)} fusion(f32[2048,1024]{1,0:T(8,128)} %param.18, f32[]{:T(128)S(6)} %copy.33), kind=kLoop, calls=%fused_computation.14 | loop fusion | flops 2097152 | bytes 16777220 | tf_op jit(solution)/shard_map/add | solution.py:42
  26.7 1.1 all-gather.4.cloned.1.call-done
  27.9 8.6 %fusion.23 = f32[768,2048]{1,0:T(8,128)} fusion(bf16[1024,2048]{1,0:T(8,128)(2,1)} %param.16, bf16[512,1024]{1,0:T(8,128)(2,1)} %all-gather.4.cloned.1.call-done, bf16[256,1024]{1,0:T(8,128)(2,1)S(1)} %all_gather.12), kind=kOutput, calls=%fused_computation.19 | convolution fusion | flops 3224371200 | bytes 12058624 | tf_op jit(solution)/shard_map/dot_general | solution.py:34
  36.5 264.8 %all-reduce.2 = bf16[768,2048]{1,0:T(8,128)(2,1)S(1)} all-reduce(f32[768,2048]{1,0:T(8,128)} %fusion.23), channel_id=1, replica_groups=mesh['row'=4,'col'=8] {'col'}, use_global_device_ids=true, to_apply=%region_0.0 | all-reduce | flops 1572864 | bytes 9437184 | tf_op jit(solution)/shard_map/psum | solution.py:35
  301.3 1.2 slice.16
  302.5 2.5 copy.17
  305.0 8.3 %fusion.19 = f32[768,1024]{1,0:T(8,128)} fusion(bf16[2048,1024]{1,0:T(8,128)(2,1)} %param.17, bf16[512,2048]{1,0:T(8,128)(2,1)} %all-gather.8.cloned.1.call-done, bf16[256,2048]{1,0:T(8,128)(2,1)} %all-gather.6.cloned.1.call-done), kind=kOutput, calls=%fused_computation.15 | convolution fusion | flops 3227516928 | bytes 10485760 | tf_op jit(solution)/shard_map/dot_general | solution.py:36
  313.3 60.3 %all-reduce.3 = bf16[768,1024]{1,0:T(8,128)(2,1)} all-reduce(f32[768,1024]{1,0:T(8,128)} %fusion.19), channel_id=1, replica_groups=mesh['row'=4,'col'=8] {'row'}, use_global_device_ids=true, to_apply=%region_1.0 | all-reduce | flops 786432 | bytes 4718592 | tf_op jit(solution)/shard_map/psum | solution.py:37
  373.6 2.9 slice_convert_fusion
  376.5 3.0 copy.18
  379.5 141.6 %while.10 = (s32[]{:T(128)}, f32[8,4,512]{2,1,0:T(4,128)S(1)}, s32[256]{0:T(256)S(1)}, s32[8]{0:T(128)S(1)}, bf16[256,2048]{0,1:T(8,128)(2,1)}, /*index=5*/bf16[...) while((s32[]{:T(128)}, f32[8,4,512]{2,1,0:T(4,128)S(1)}, ...), condition=%wide.region_4.5_spmd, body=%wide.region_2.4_spmd.sunk | while | flops 12907970560 | bytes 14185625 | solution.py:62
  380.1 0.6 iota_add_fusion.2
  380.9 16.4 %fusion.42 = f32[512,4]{0,1:T(4,128)S(1)} fusion(f32[512,1024]{0,1:T(8,128)} %get-tuple-element.178, bf16[512,2048]{1,0:T(8,128)(2,1)S(1)} %get-tuple-element.177, f32[2048,1024]{1,0:T(8,128)} %get-tuple-element.176, bf16[256,2048]{0,1:T(8,128)(2,1)} %get-tuple-element.174, bf16[256,4]{0,1:T(4,128)(2,1)S(1)} %compare_convert_fusion.2, ...), kind=kOutput, calls=%fused_computation.4.clone.1 | convolution fusion | flops 12907968512 | bytes 14166016 | tf_op jit(solution)/shard_map/while/body/eval_jaxpr/ui,sij->usj/dot_general | solution.py:58
  397.9 0.6 iota_add_fusion.2
  398.6 16.4 %fusion.42 = f32[512,4]{0,1:T(4,128)S(1)} fusion(f32[512,1024]{0,1:T(8,128)} %get-tuple-element.178, bf16[512,2048]{1,0:T(8,128)(2,1)S(1)} %get-tuple-element.177, f32[2048,1024]{1,0:T(8,128)} %get-tuple-element.176, bf16[256,2048]{0,1:T(8,128)(2,1)} %get-tuple-element.174, bf16[256,4]{0,1:T(4,128)(2,1)S(1)} %compare_convert_fusion.2, ...), kind=kOutput, calls=%fused_computation.4.clone.1 | convolution fusion | flops 12907968512 | bytes 14166016 | tf_op jit(solution)/shard_map/while/body/eval_jaxpr/ui,sij->usj/dot_general | solution.py:58
  415.6 0.6 iota_add_fusion.2
  416.3 16.4 %fusion.42 = f32[512,4]{0,1:T(4,128)S(1)} fusion(f32[512,1024]{0,1:T(8,128)} %get-tuple-element.178, bf16[512,2048]{1,0:T(8,128)(2,1)S(1)} %get-tuple-element.177, f32[2048,1024]{1,0:T(8,128)} %get-tuple-element.176, bf16[256,2048]{0,1:T(8,128)(2,1)} %get-tuple-element.174, bf16[256,4]{0,1:T(4,128)(2,1)S(1)} %compare_convert_fusion.2, ...), kind=kOutput, calls=%fused_computation.4.clone.1 | convolution fusion | flops 12907968512 | bytes 14166016 | tf_op jit(solution)/shard_map/while/body/eval_jaxpr/ui,sij->usj/dot_general | solution.py:58
  434.0 16.4 %fusion.42 = f32[512,4]{0,1:T(4,128)S(1)} fusion(f32[512,1024]{0,1:T(8,128)} %get-tuple-element.178, bf16[512,2048]{1,0:T(8,128)(2,1)S(1)} %get-tuple-element.177, f32[2048,1024]{1,0:T(8,128)} %get-tuple-element.176, bf16[256,2048]{0,1:T(8,128)(2,1)} %get-tuple-element.174, bf16[256,4]{0,1:T(4,128)(2,1)S(1)} %compare_convert_fusion.2, ...), kind=kOutput, calls=%fused_computation.4.clone.1 | convolution fusion | flops 12907968512 | bytes 14166016 | tf_op jit(solution)/shard_map/while/body/eval_jaxpr/ui,sij->usj/dot_general | solution.py:58
  451.7 16.4 %fusion.42 = f32[512,4]{0,1:T(4,128)S(1)} fusion(f32[512,1024]{0,1:T(8,128)} %get-tuple-element.178, bf16[512,2048]{1,0:T(8,128)(2,1)S(1)} %get-tuple-element.177, f32[2048,1024]{1,0:T(8,128)} %get-tuple-element.176, bf16[256,2048]{0,1:T(8,128)(2,1)} %get-tuple-element.174, bf16[256,4]{0,1:T(4,128)(2,1)S(1)} %compare_convert_fusion.2, ...), kind=kOutput, calls=%fused_computation.4.clone.1 | convolution fusion | flops 12907968512 | bytes 14166016 | tf_op jit(solution)/shard_map/while/body/eval_jaxpr/ui,sij->usj/dot_general | solution.py:58
  469.4 16.4 %fusion.42 = f32[512,4]{0,1:T(4,128)S(1)} fusion(f32[512,1024]{0,1:T(8,128)} %get-tuple-element.178, bf16[512,2048]{1,0:T(8,128)(2,1)S(1)} %get-tuple-element.177, f32[2048,1024]{1,0:T(8,128)} %get-tuple-element.176, bf16[256,2048]{0,1:T(8,128)(2,1)} %get-tuple-element.174, bf16[256,4]{0,1:T(4,128)(2,1)S(1)} %compare_convert_fusion.2, ...), kind=kOutput, calls=%fused_computation.4.clone.1 | convolution fusion | flops 12907968512 | bytes 14166016 | tf_op jit(solution)/shard_map/while/body/eval_jaxpr/ui,sij->usj/dot_general | solution.py:58
  487.1 16.4 %fusion.42 = f32[512,4]{0,1:T(4,128)S(1)} fusion(f32[512,1024]{0,1:T(8,128)} %get-tuple-element.178, bf16[512,2048]{1,0:T(8,128)(2,1)S(1)} %get-tuple-element.177, f32[2048,1024]{1,0:T(8,128)} %get-tuple-element.176, bf16[256,2048]{0,1:T(8,128)(2,1)} %get-tuple-element.174, bf16[256,4]{0,1:T(4,128)(2,1)S(1)} %compare_convert_fusion.2, ...), kind=kOutput, calls=%fused_computation.4.clone.1 | convolution fusion | flops 12907968512 | bytes 14166016 | tf_op jit(solution)/shard_map/while/body/eval_jaxpr/ui,sij->usj/dot_general | solution.py:58
  504.8 16.4 %fusion.42 = f32[512,4]{0,1:T(4,128)S(1)} fusion(f32[512,1024]{0,1:T(8,128)} %get-tuple-element.178, bf16[512,2048]{1,0:T(8,128)(2,1)S(1)} %get-tuple-element.177, f32[2048,1024]{1,0:T(8,128)} %get-tuple-element.176, bf16[256,2048]{0,1:T(8,128)(2,1)} %get-tuple-element.174, bf16[256,4]{0,1:T(4,128)(2,1)S(1)} %compare_convert_fusion.2, ...), kind=kOutput, calls=%fused_computation.4.clone.1 | convolution fusion | flops 12907968512 | bytes 14166016 | tf_op jit(solution)/shard_map/while/body/eval_jaxpr/ui,sij->usj/dot_general | solution.py:58
  521.3 0.8 copy.20
  522.3 58.0 %reduce-scatter.4.cloned.1.call-done = f32[64,32]{1,0:T(8,128)} async-done(((f32[512,32]{1,0:T(8,128)}), f32[64,32]{1,0:T(8,128)}) %reduce-scatter.4.cloned.1.call-update) | async-done | bytes 8208
  580.2 0.8 copy.21
  581.1 11.6 %psum.30 = f32[32,64]{1,0:T(8,128)S(1)} all-reduce(f32[32,64]{1,0:T(8,128)S(1)} %copy.21), channel_id=1, replica_groups=mesh['row'=4,'col'=8] {'row'}, use_global_device_ids=true, to_apply=%region_6.7 | all-reduce | flops 2048 | bytes 16384 | tf_op jit(solution)/shard_map/psum | solution.py:70
  592.9 11.5 %psum.31 = f32[32,16]{0,1:T(8,128)S(1)} all-reduce(f32[32,16]{0,1:T(8,128)S(1)} %fusion.27), channel_id=1, replica_groups=mesh['row'=4,'col'=8] {'col'}, use_global_device_ids=true, to_apply=%region_7.8 | all-reduce | flops 512 | bytes 4096 | tf_op jit(solution)/shard_map/psum | solution.py:73
  604.4 0.7 broadcast_divide_fusion
  (55 shorter events, 9.2 us)
Async XLA Ops:
  7.2 20.7 %all-gather.4.cloned.1.call-start = ((), (), s32[]{:S(2)}) async-start(), calls=%async_computation.1 | async-start | bytes 1310720 | tf_op jit(solution)/shard_map/all_gather | solution.py:25
  7.9 297.1 %all-gather.6.cloned.1.call-start = ((), (), s32[]{:S(2)}) async-start(), calls=%async_computation.2 | async-start | bytes 1179648 | tf_op jit(solution)/shard_map/all_gather | solution.py:28
  8.6 296.3 %all-gather.8.cloned.1.call-start = ((), (), s32[]{:S(2)}) async-start(), calls=%async_computation.3 | async-start | bytes 2359296 | tf_op jit(solution)/shard_map/all_gather | solution.py:29
  9.4 570.9 %reduce-scatter.4.cloned.1.call-start = ((), (), s32[]{:S(2)}) async-start(), calls=%async_computation.4 | async-start | bytes 294912
  301.3 12.0 %copy-start = (bf16[768,2048]{1,0:T(8,128)(2,1)}, bf16[768,2048]{1,0:T(8,128)(2,1)S(1)}, u32[]{:S(2)}) copy-start(bf16[768,2048]{1,0:T(8,128)(2,1)S(1)} %all-reduce.2) | copy-start | bytes 9437188
  373.6 5.9 slice-start
  373.6 5.9 slice-start.1
  373.6 5.9 copy-start.2
  379.5 142.6 %copy-start.3 = (s32[512]{0:T(512)S(1)}, s32[512]{0:T(512)}, u32[]{:S(2)}) copy-start(s32[512]{0:T(512)} %param.21) | copy-start | bytes 6148
  592.7 12.4 %copy-start.1 = (f32[32,64]{1,0:T(8,128)}, f32[32,64]{1,0:T(8,128)S(1)}, u32[]{:S(2)}) copy-start(f32[32,64]{1,0:T(8,128)S(1)} %psum.30) | copy-start | bytes 24580
Sparse Core Ops, SparseCore 0:
  9.6 18.2 all-gather.3
  30.0 58.9 all-gather.5
  91.1 86.0 all-gather.7
  522.2 57.9 reduce-scatter.3
where the time goes:
time: 622 us; the launch traced here: 612 us
  blocking collectives  356 us (57%)
  matrix products  148 us (24%)
  waiting for transfers between devices  61.2 us (10%)
  other arithmetic  18.2 us (3%)
  between operations  14.5 us (2%)
  local copies, waits for them, and re-layouts  13.2 us (2%)
    psum x1, blocking collectives, local(): grads_rot = lax.psum(grad_part, 'col').astype(jnp.bfloat16)  265 us
    dot_general x8, matrix products, score_group(): jnp.einsum('ui,sij->usj', rot_gu, precond, preferred_element_type=jnp.flo...  131 us
    psum x1, blocking collectives, local(): acts_rot = lax.psum(act_part, 'row').astype(jnp.bfloat16)  60.3 us
    unnamed x5, waiting for transfers between devices  60.1 us
  transfers between devices with their start and end apart: 4, of which 2 were waited for; matrix products, arithmetic and copies ran while one was open for 3% of the time, Pallas kernels for 0%

commit v1 on v0

v1 whole, which is shorter than its diff:
```python
import functools

import jax
import jax.numpy as jnp
from jax import lax
from jax.experimental import pallas as pl
from jax.experimental.pallas import tpu as pltpu
from jax.sharding import PartitionSpec as P

D = 8192
S = 32
DOCS = 16
CHUNKS = 4


def score_kernel(n_seq, n_query, sub, damp_ref, seq_ref, grad_ref, aq_ref, au_ref, eig_ref, out_ref,
                 inv_ref, wide_ref, even_ref, odd_ref):
    rows, cols = eig_ref.shape
    n_train = au_ref.shape[1]
    inv_ref[...] = 1.0 / (eig_ref[...] + damp_ref[0, 0])
    wide_ref[...] = grad_ref[:, n_query:].astype(jnp.float32)

    def precondition(s, p_ref):
        member = (seq_ref[...] == s).astype(jnp.float32).astype(jnp.bfloat16)
        acts = aq_ref[...] * member
        for first in range(0, rows, sub):
            span = pl.ds(first, sub)
            outer = jnp.dot(grad_ref[span, :n_query], acts, preferred_element_type=jnp.float32)
            p_ref[span, :] = (outer * inv_ref[span, :]).astype(jnp.bfloat16)

    def score(s, p_ref):
        total = jnp.zeros((8, n_train), jnp.float32)
        for first in range(0, rows, sub):
            span = pl.ds(first, sub)
            mapped = jnp.dot(p_ref[span, :], au_ref[...], preferred_element_type=jnp.float32)
            weighted = mapped * wide_ref[span, :]
            total = total + jnp.sum(weighted.reshape(sub // 8, 8, n_train), axis=0)
        out_ref[pl.ds(s, 1), :] = jnp.sum(total, axis=0, keepdims=True)

    precondition(0, even_ref)

    def pair(k, carry):
        precondition(2 * k + 1, odd_ref)
        score(2 * k, even_ref)
        precondition(2 * k + 2, even_ref)
        score(2 * k + 1, odd_ref)
        return carry

    lax.fori_loop(0, n_seq // 2, pair, 0)


def score_chunk(damping, seq, grads_t, acts_q, acts_ut, eig):
    rows, cols = eig.shape
    n_query, n_train = acts_q.shape[0], acts_ut.shape[1]
    sub = min(rows, 512)
    flops = 2 * S * rows * cols * (n_query + n_train)
    return pl.pallas_call(
        functools.partial(score_kernel, S, n_query, sub),
        out_shape=jax.ShapeDtypeStruct((S, n_train), jnp.float32),
        in_specs=[pl.BlockSpec(memory_space=pltpu.SMEM)]
        + [pl.BlockSpec(memory_space=pltpu.VMEM)] * 5,
        out_specs=pl.BlockSpec(memory_space=pltpu.VMEM),
        scratch_shapes=[
            pltpu.VMEM((rows, cols), jnp.float32),
            pltpu.VMEM((rows, n_train), jnp.float32),
            pltpu.VMEM((rows, cols), jnp.bfloat16),
            pltpu.VMEM((rows, cols), jnp.bfloat16),
        ],
        compiler_params=pltpu.CompilerParams(vmem_limit_bytes=48 * 1024 * 1024),
        cost_estimate=pl.CostEstimate(
            flops=flops, bytes_accessed=rows * cols * 4, transcendentals=0
        ),
    )(damping, seq, grads_t, acts_q, acts_ut, eig)


def local(
    query_grads,
    query_acts,
    train_grads,
    train_acts,
    grad_basis,
    act_basis,
    eigen_corr,
    damping,
    query_seq,
    train_doc,
):
    f32, bf16 = jnp.float32, jnp.bfloat16
    gather = functools.partial(lax.all_gather, axis=0, tiled=True)
    acts_all = jnp.concatenate([gather(query_acts, "col"), gather(train_acts, "col")], axis=0)
    grads_all = jnp.concatenate([gather(query_grads, "row"), gather(train_grads, "row")], axis=0)
    n_col = lax.axis_size("col")
    n_query = query_seq.shape[0]
    row_block, col_block = eigen_corr.shape

    act_part = jnp.dot(acts_all, act_basis, preferred_element_type=f32)
    act_own = lax.psum_scatter(act_part, "row", scatter_dimension=0, tiled=True).astype(bf16)
    acts_rot = gather(act_own, "row")
    acts_q, acts_ut = acts_rot[:n_query], acts_rot[n_query:].T

    damp = damping.reshape(1, 1)
    seq = query_seq.reshape(n_query, 1)
    step = row_block // CHUNKS
    partial_scores = 0.0
    for chunk in range(CHUNKS):
        basis = grad_basis[:, chunk * step : (chunk + 1) * step]
        part = lax.dot_general(
            basis, grads_all, (((0,), (1,)), ((), ())), preferred_element_type=f32
        )
        own = lax.psum_scatter(part, "col", scatter_dimension=0, tiled=True).astype(bf16)
        grads_t = gather(own, "col")
        eig = eigen_corr[chunk * step : (chunk + 1) * step]
        partial_scores = partial_scores + score_chunk(damp, seq, grads_t, acts_q, acts_ut, eig)
    partial_scores = partial_scores / D

    doc_table = (train_doc[:, None] == jnp.arange(DOCS, dtype=jnp.int32)[None, :]).astype(f32)
    counts = jnp.sum(doc_table, axis=0)
    total = lax.psum(partial_scores, ("row", "col"))
    owned = total.shape[1] // n_col
    scores = lax.dynamic_slice_in_dim(total, lax.axis_index("col") * owned, owned, 1)
    doc_sum = jnp.dot(total, doc_table, precision=lax.Precision.HIGHEST)
    return (scores, doc_sum / counts[None, :])


def solution(mesh):
    in_specs = (
        P("row", "col"),
        P("col", "row"),
        P("row", "col"),
        P("col", "row"),
        P("col", "row"),
        P("row", "col"),
        P("row", "col"),
        P(),
        P(),
        P(),
    )
    out_specs = (P(None, "col"), P())
    return jax.shard_map(local, mesh=mesh, in_specs=in_specs, out_specs=out_specs, check_vma=False)
```

time: 622 us -> 830 us (1.33)
  waiting for transfers between devices: 61.2 us -> 518 us
  blocking collectives: 356 us -> 122 us
  matrix products: 148 us -> 23.7 us
  Pallas kernels: 0 us -> 123 us
  other arithmetic: 18.2 us -> 6.45 us
    psum x4 -> x0, blocking collectives: 348 us -> none  [the longest x1 265 us: local(): grads_rot = lax.psum(grad_part, 'col').astype(jnp.bfloat16)]
    reduce_scatter x0 -> x5, waiting for transfers between devices: none -> 281 us  [the longest x4 256 us: local(): lax.psum_scatter(part, 'col', scatter_dimension=0, tiled=True).astype(bf16)]
    psum x0 -> x1, waiting for transfers between devices: none -> 144 us  [local(): total = lax.psum(partial_scores, ('row', 'col'))]
    dot_general x11 -> x5, matrix products: 148 us -> 15.4 us  [the longest x4 13.8 us: local(): lax.dot_general(basis, grads_all, (((0,), (1,)), ((), ())), preferred_ele...]
    pallas_call x0 -> x4, Pallas kernels: none -> 123 us  [score_chunk(): pl.pallas_call(functools.partial(score_kernel, S, n_query, sub), out_shap...]
    all_gather x1 -> x5, blocking collectives: 7.92 us -> 122 us  [the longest x4 110 us: local(): grads_t = gather(own, 'col')]
    all_gather x3 -> x4, waiting for transfers between devices: 1.15 us -> 91.3 us  [the longest x1 51 us: local(): gather(train_acts, 'col')]
    unnamed x5 -> x10, waiting for transfers between devices: 60.1 us -> 2.17 us
  transfers between devices with their start and end apart: 4 -> 10, of which waited for: 2 -> 9; matrix products, arithmetic and copies ran while one was open for 3% -> 4% of each run, Pallas kernels for 0% -> 0%
where the time goes in v1:
time: 830 us; the launch traced here: 827 us
  waiting for transfers between devices  518 us (62%)
  Pallas kernels  123 us (15%)
  blocking collectives  122 us (15%)
  matrix products  23.7 us (3%)
  local copies, waits for them, and re-layouts  17.9 us (2%)
  between operations  15 us (2%)
    reduce_scatter x4, waiting for transfers between devices, local(): lax.psum_scatter(part, 'col', scatter_dimension=0, tiled=True).astype(bf16)  256 us
    psum x1, waiting for transfers between devices, local(): total = lax.psum(partial_scores, ('row', 'col'))  144 us
    pallas_call x4, Pallas kernels, score_chunk(): pl.pallas_call(functools.partial(score_kernel, S, n_query, sub), out_shap...  123 us
    all_gather x4, blocking collectives, local(): grads_t = gather(own, 'col')  110 us
    all_gather x1, waiting for transfers between devices, local(): gather(train_acts, 'col')  51 us
    all_gather x1, waiting for transfers between devices, local(): gather(query_acts, 'col')  39.5 us
    reduce_scatter x1, waiting for transfers between devices, local(): lax.psum_scatter(act_part, 'row', scatter_dimension=0, tiled=True)  24.5 us
  transfers between devices with their start and end apart: 10, of which 9 were waited for; matrix products, arithmetic and copies ran while one was open for 4% of the time, Pallas kernels for 0%

profile of v1, /device:TPU:11, one launch (start us, length us, event | category | flops | bytes accessed | tf_op | source)
XLA Modules:
  0.0 826.6 jit_solution(6217470701702219609)
XLA Ops:
  9.4 39.5 %all-gather.7.cloned.1.call-done = bf16[256,2048]{1,0:T(8,128)(2,1)} async-done(((bf16[32,2048]{1,0:T(8,128)(2,1)}), bf16[256,2048]{1,0:T(8,128)(2,1)}) %all-gather.7.cloned.1.call-update) | async-done | bytes 1048592 | tf_op jit(solution)/shard_map/all_gather | solution.py:90
  48.9 51.0 %all-gather.9.cloned.1.call-done = bf16[512,2048]{1,0:T(8,128)(2,1)} async-done(((bf16[64,2048]{1,0:T(8,128)(2,1)}), bf16[512,2048]{1,0:T(8,128)(2,1)}) %all-gather.9.cloned.1.call-update) | async-done | bytes 2097168 | tf_op jit(solution)/shard_map/all_gather | solution.py:90
  99.9 8.2 fusion
  109.0 11.8 %all_gather.27 = bf16[256,1024]{1,0:T(8,128)(2,1)S(1)} all-gather(bf16[64,1024]{1,0:T(8,128)(2,1)S(1)} %copy-done.7), channel_id=1, replica_groups=mesh['row'=4,'col'=8] {'row'}, dimensions={0}, use_global_device_ids=true | all-gather | bytes 655360 | tf_op jit(solution)/shard_map/all_gather | solution.py:91
  121.7 1.3 constant_dynamic-update-slice_fusion
  123.0 3.5 convolution_bitcast_fusion
  126.6 3.4 convolution_bitcast_fusion.1
  130.0 3.4 convolution_bitcast_fusion.3
  133.5 3.5 convolution_bitcast_fusion.2
  137.1 24.5 %reduce-scatter.16.cloned.1.call-done = f32[192,1024]{1,0:T(8,128)} async-done(((f32[768,1024]{1,0:T(8,128)}), f32[192,1024]{1,0:T(8,128)}) %reduce-scatter.16.cloned.1.call-update) | async-done | bytes 786448 | tf_op jit(solution)/shard_map/reduce_scatter | solution.py:97
  161.6 1.9 convert_element_type.19
  164.4 6.6 fusion.10
  171.1 57.1 %reduce-scatter.14.cloned.1.call-done = f32[64,768]{1,0:T(8,128)} async-done(((f32[512,768]{1,0:T(8,128)}), f32[64,768]{1,0:T(8,128)}) %reduce-scatter.14.cloned.1.call-update) | async-done | bytes 196624 | tf_op jit(solution)/shard_map/reduce_scatter | solution.py:110
  229.1 66.1 %reduce-scatter.12.cloned.1.call-done = f32[64,768]{1,0:T(8,128)} async-done(((f32[512,768]{1,0:T(8,128)}), f32[64,768]{1,0:T(8,128)}) %reduce-scatter.12.cloned.1.call-update) | async-done | bytes 196624 | tf_op jit(solution)/shard_map/reduce_scatter | solution.py:110
  296.2 66.6 %reduce-scatter.8.cloned.1.call-done = f32[64,768]{1,0:T(8,128)} async-done(((f32[512,768]{1,0:T(8,128)}), f32[64,768]{1,0:T(8,128)}) %reduce-scatter.8.cloned.1.call-update) | async-done | bytes 196624 | tf_op jit(solution)/shard_map/reduce_scatter | solution.py:110
  363.8 66.3 %reduce-scatter.10.cloned.1.call-done = f32[64,768]{1,0:T(8,128)} async-done(((f32[512,768]{1,0:T(8,128)}), f32[64,768]{1,0:T(8,128)}) %reduce-scatter.10.cloned.1.call-update) | async-done | bytes 196624 | tf_op jit(solution)/shard_map/reduce_scatter | solution.py:110
  431.0 24.3 %all_gather.35.grad_ref = bf16[512,768]{1,0:T(8,128)(2,1)} all-gather(bf16[64,768]{1,0:T(8,128)(2,1)S(1)} %convert_element_type.22), channel_id=1, replica_groups=mesh['row'=4,'col'=8] {'col'}, dimensions={0}, use_global_device_ids=true | all-gather | bytes 884736 | tf_op jit(solution)/shard_map/all_gather | solution.py:111
  455.4 28.9 %all_gather.34.grad_ref = bf16[512,768]{1,0:T(8,128)(2,1)} all-gather(bf16[64,768]{1,0:T(8,128)(2,1)S(1)} %convert_element_type.21), channel_id=1, replica_groups=mesh['row'=4,'col'=8] {'col'}, dimensions={0}, use_global_device_ids=true | all-gather | bytes 884736 | tf_op jit(solution)/shard_map/all_gather | solution.py:111
  484.3 28.7 %all_gather.29.grad_ref = bf16[512,768]{1,0:T(8,128)(2,1)} all-gather(bf16[64,768]{1,0:T(8,128)(2,1)S(1)} %convert_element_type.18), channel_id=1, replica_groups=mesh['row'=4,'col'=8] {'col'}, dimensions={0}, use_global_device_ids=true | all-gather | bytes 884736 | tf_op jit(solution)/shard_map/all_gather | solution.py:111
  513.0 28.3 %all_gather.33.grad_ref = bf16[512,768]{1,0:T(8,128)(2,1)} all-gather(bf16[64,768]{1,0:T(8,128)(2,1)S(1)} %convert_element_type.20), channel_id=1, replica_groups=mesh['row'=4,'col'=8] {'col'}, dimensions={0}, use_global_device_ids=true | all-gather | bytes 884736 | tf_op jit(solution)/shard_map/all_gather | solution.py:111
  541.3 2.3 slice.41
  543.6 1.5 copy.74
  545.1 1.1 slice.40.aq_ref
  546.2 1.6 copy-done.2
  547.8 1.1 copy-done.6
  548.9 30.7 %shard_map.116 = f32[32,512]{1,0:T(8,128)S(1)} custom-call(f32[1,1]{1,0:T(1,128)} %bitcast.21.damp_ref, s32[256,1]{1,0:T(8,128)S(1)} %copy.60.seq_ref, bf16[512,768]{1,0:T(8,128)(2,1)S(1)} %copy-done.6, bf16[256,1024]{1,0:T(8,128)(2,1)S(1)} %slice.40.aq_ref, bf16[1024,512]{1,0:T(8,128)(2,1)S(1)} %bitcast.22, f32[512,1024]{1,0:T(8,128)S(1)} %copy-done.2), custom_call_target="tpu_custom_call" | custom-call | flops 25769803776 | bytes 2097152 | tf_op jit(solution)/shard_map/pallas_call | solution.py:57
  579.6 30.7 %shard_map.115 = f32[32,512]{1,0:T(8,128)S(1)} custom-call(f32[1,1]{1,0:T(1,128)} %bitcast.20.damp_ref, s32[256,1]{1,0:T(8,128)S(1)} %copy.60.seq_ref, bf16[512,768]{1,0:T(8,128)(2,1)S(1)} %copy-done.5, bf16[256,1024]{1,0:T(8,128)(2,1)S(1)} %slice.40.aq_ref, bf16[1024,512]{1,0:T(8,128)(2,1)S(1)} %bitcast.23, f32[512,1024]{1,0:T(8,128)S(1)} %copy-done.1), custom_call_target="tpu_custom_call" | custom-call | flops 25769803776 | bytes 2097152 | tf_op jit(solution)/shard_map/pallas_call | solution.py:57
  610.3 30.7 %shard_map.113 = f32[32,512]{1,0:T(8,128)S(1)} custom-call(f32[1,1]{1,0:T(1,128)} %bitcast.18.damp_ref, s32[256,1]{1,0:T(8,128)S(1)} %copy.60.seq_ref, bf16[512,768]{1,0:T(8,128)(2,1)S(1)} %copy-done.4, bf16[256,1024]{1,0:T(8,128)(2,1)S(1)} %slice.40.aq_ref, bf16[1024,512]{1,0:T(8,128)(2,1)S(1)} %bitcast.24, f32[512,1024]{1,0:T(8,128)S(1)} %copy-done), custom_call_target="tpu_custom_call" | custom-call | flops 25769803776 | bytes 2097152 | tf_op jit(solution)/shard_map/pallas_call | solution.py:57
  641.0 30.7 %shard_map.114 = f32[32,512]{1,0:T(8,128)S(1)} custom-call(f32[1,1]{1,0:T(1,128)} %bitcast.19.damp_ref, s32[256,1]{1,0:T(8,128)S(1)} %copy.60.seq_ref, bf16[512,768]{1,0:T(8,128)(2,1)S(1)} %copy-done.3, bf16[256,1024]{1,0:T(8,128)(2,1)S(1)} %slice.40.aq_ref, bf16[1024,512]{1,0:T(8,128)(2,1)S(1)} %bitcast.25, f32[512,1024]{1,0:T(8,128)S(1)} %get-tuple-element.2.eig_ref), custom_call_target="tpu_custom_call" | custom-call | flops 25769803776 | bytes 2097152 | tf_op jit(solution)/shard_map/pallas_call | solution.py:57
  672.5 144.3 %all-reduce.2.cloned.1.call-done = f32[32,512]{1,0:T(8,128)} async-done(((f32[32,512]{1,0:T(8,128)}), f32[32,512]{1,0:T(8,128)}) %all-reduce.2.cloned.1.call-update) | async-done | bytes 65552 | tf_op jit(solution)/shard_map/psum | solution.py:118
  816.8 1.4 constant_dynamic-slice_fusion
  818.2 1.6 convolution_divide_fusion
  (48 shorter events, 8.9 us)
Async XLA Ops:
  7.2 41.7 %all-gather.7.cloned.1.call-start = ((), (), s32[]{:S(2)}) async-start(), calls=%async_computation.7 | async-start | bytes 1179648 | tf_op jit(solution)/shard_map/all_gather | solution.py:90
  7.9 92.0 %all-gather.9.cloned.1.call-start = ((), (), s32[]{:S(2)}) async-start(), calls=%async_computation.8 | async-start | bytes 2359296 | tf_op jit(solution)/shard_map/all_gather | solution.py:90
  8.6 113.0 %all-gather.5.cloned.1.call-start = ((), (), s32[]{:S(2)}) async-start(), calls=%async_computation.5 | async-start | bytes 1310720 | tf_op jit(solution)/shard_map/all_gather | solution.py:91
  9.4 152.2 %reduce-scatter.16.cloned.1.call-start = ((), (), s32[]{:S(2)}) async-start(), calls=%async_computation.14 | async-start | bytes 3932160 | tf_op jit(solution)/shard_map/reduce_scatter | solution.py:97
  108.1 0.9 copy-start.7
  108.1 120.1 %reduce-scatter.14.cloned.1.call-start = ((), (), s32[]{:S(2)}) async-start(), calls=%async_computation.12 | async-start | bytes 1769472 | tf_op jit(solution)/shard_map/reduce_scatter | solution.py:110
  126.5 168.8 %reduce-scatter.12.cloned.1.call-start = ((), (), s32[]{:S(2)}) async-start(), calls=%async_computation.11 | async-start | bytes 1769472 | tf_op jit(solution)/shard_map/reduce_scatter | solution.py:110
  130.0 232.8 %reduce-scatter.8.cloned.1.call-start = ((), (), s32[]{:S(2)}) async-start(), calls=%async_computation.6 | async-start | bytes 1769472 | tf_op jit(solution)/shard_map/reduce_scatter | solution.py:110
  133.5 296.6 %reduce-scatter.10.cloned.1.call-start = ((), (), s32[]{:S(2)}) async-start(), calls=%async_computation.10 | async-start | bytes 1769472 | tf_op jit(solution)/shard_map/reduce_scatter | solution.py:110
  137.0 27.3 %copy-start.9 = (s32[256]{0:T(256)S(1)}, s32[256]{0:T(256)}, u32[]{:S(2)}) copy-start(s32[256]{0:T(256)} %param.18) | copy-start | bytes 3076
  137.1 404.2 %all-gather.11.cloned.1.call-start = ((), (), s32[]{:S(2)}) async-start(), calls=%async_computation.9 | async-start | bytes 1966080 | tf_op jit(solution)/shard_map/all_gather | solution.py:98
  163.6 653.2 %all-reduce.2.cloned.1.call-start = ((), (), s32[]{:S(2)}) async-start(), calls=%async_computation.13 | async-start | bytes 131072 | tf_op jit(solution)/shard_map/psum | solution.py:118
  546.2 1.6 copy-start.2
  547.8 1.1 copy-start.6
  548.9 30.7 %copy-start.1 = (f32[512,1024]{1,0:T(8,128)S(1)}, f32[512,1024]{1,0:T(8,128)}, u32[]{:S(2)}) copy-start(f32[512,1024]{1,0:T(8,128)} %get-tuple-element.5.eig_ref) | copy-start | bytes 6291460
  548.9 30.7 %copy-start.5 = (bf16[512,768]{1,0:T(8,128)(2,1)S(1)}, bf16[512,768]{1,0:T(8,128)(2,1)}, u32[]{:S(2)}) copy-start(bf16[512,768]{1,0:T(8,128)(2,1)} %all_gather.34.grad_ref) | copy-start | bytes 2359300
  579.6 30.7 %copy-start = (f32[512,1024]{1,0:T(8,128)S(1)}, f32[512,1024]{1,0:T(8,128)}, u32[]{:S(2)}) copy-start(f32[512,1024]{1,0:T(8,128)} %get-tuple-element.3.eig_ref) | copy-start | bytes 6291460
  579.6 30.7 %copy-start.4 = (bf16[512,768]{1,0:T(8,128)(2,1)S(1)}, bf16[512,768]{1,0:T(8,128)(2,1)}, u32[]{:S(2)}) copy-start(bf16[512,768]{1,0:T(8,128)(2,1)} %all_gather.29.grad_ref) | copy-start | bytes 2359300
  610.3 30.7 %copy-start.3 = (bf16[512,768]{1,0:T(8,128)(2,1)S(1)}, bf16[512,768]{1,0:T(8,128)(2,1)}, u32[]{:S(2)}) copy-start(bf16[512,768]{1,0:T(8,128)(2,1)} %all_gather.33.grad_ref) | copy-start | bytes 2359300
  641.0 31.3 %copy-start.8 = (s32[512]{0:T(512)S(1)}, s32[512]{0:T(512)}, u32[]{:S(2)}) copy-start(s32[512]{0:T(512)} %param.19) | copy-start | bytes 6148
Sparse Core Ops, SparseCore 0:
  10.1 38.7 all-gather.6
  51.0 48.8 all-gather.8
  101.5 20.1 all-gather.4
  124.1 37.5 reduce-scatter.15
  165.3 62.8 reduce-scatter.13
  231.5 63.7 reduce-scatter.11
  299.1 63.6 reduce-scatter.7
  366.2 63.7 reduce-scatter.9
  431.7 20.9 all-gather.10
  672.4 144.3 all-reduce.1

commit v2 on v1

v2 whole, which is shorter than its diff:
```python
import functools

import jax
import jax.numpy as jnp
from jax import lax
from jax.experimental import pallas as pl
from jax.experimental.pallas import tpu as pltpu
from jax.sharding import PartitionSpec as P

D = 8192
S = 32
DOCS = 16
CHUNKS = 4


def score_kernel(n_seq, n_query, sub, damp_ref, seq_ref, grad_ref, aq_ref, au_ref, eig_ref, out_ref,
                 inv_ref, wide_ref, even_ref, odd_ref):
    rows, cols = eig_ref.shape
    n_train = au_ref.shape[1]
    @pl.when(pl.program_id(0) == 0)
    def _():
        out_ref[...] = jnp.zeros_like(out_ref)

    inv_ref[...] = 1.0 / (eig_ref[...] + damp_ref[0, 0])
    wide_ref[...] = grad_ref[:, n_query:].astype(jnp.float32)

    def precondition(s, p_ref):
        member = (seq_ref[...] == s).astype(jnp.float32).astype(jnp.bfloat16)
        acts = aq_ref[...] * member
        for first in range(0, rows, sub):
            span = pl.ds(first, sub)
            outer = jnp.dot(grad_ref[span, :n_query], acts, preferred_element_type=jnp.float32)
            p_ref[span, :] = (outer * inv_ref[span, :]).astype(jnp.bfloat16)

    def score(s, p_ref):
        total = jnp.zeros((8, n_train), jnp.float32)
        for first in range(0, rows, sub):
            span = pl.ds(first, sub)
            mapped = jnp.dot(p_ref[span, :], au_ref[...], preferred_element_type=jnp.float32)
            weighted = mapped * wide_ref[span, :]
            total = total + jnp.sum(weighted.reshape(sub // 8, 8, n_train), axis=0)
        out_ref[pl.ds(s, 1), :] += jnp.sum(total, axis=0, keepdims=True)

    precondition(0, even_ref)

    def pair(k, carry):
        precondition(2 * k + 1, odd_ref)
        score(2 * k, even_ref)
        precondition(2 * k + 2, even_ref)
        score(2 * k + 1, odd_ref)
        return carry

    lax.fori_loop(0, n_seq // 2, pair, 0)


def block_scores(damping, seq, grads_t, acts_q, acts_ut, eig):
    rows, cols = eig.shape
    n_query, n_train = acts_q.shape[0], acts_ut.shape[1]
    step = rows // CHUNKS
    flops = 2 * S * rows * cols * (n_query + n_train)
    whole = lambda x: pl.BlockSpec(x.shape, lambda i: (0, 0))
    part = lambda x: pl.BlockSpec((step, x.shape[1]), lambda i: (i, 0))
    return pl.pallas_call(
        functools.partial(score_kernel, S, n_query, min(step, 512)),
        grid=(CHUNKS,),
        out_shape=jax.ShapeDtypeStruct((S, n_train), jnp.float32),
        in_specs=[
            pl.BlockSpec(memory_space=pltpu.SMEM),
            whole(seq),
            part(grads_t),
            whole(acts_q),
            whole(acts_ut),
            part(eig),
        ],
        out_specs=pl.BlockSpec((S, n_train), lambda i: (0, 0)),
        scratch_shapes=[
            pltpu.VMEM((step, cols), jnp.float32),
            pltpu.VMEM((step, n_train), jnp.float32),
            pltpu.VMEM((step, cols), jnp.bfloat16),
            pltpu.VMEM((step, cols), jnp.bfloat16),
        ],
        compiler_params=pltpu.CompilerParams(vmem_limit_bytes=48 * 1024 * 1024),
        cost_estimate=pl.CostEstimate(
            flops=flops, bytes_accessed=rows * cols * 4, transcendentals=0
        ),
    )(damping, seq, grads_t, acts_q, acts_ut, eig)


MESH = pl.DeviceIdType.MESH


def ring_place(axis, n):
    me = lax.axis_index(axis)
    odd = lax.rem(me, 2)
    place = (1 - odd) * (me // 2) + odd * ((2 * n - 1 - me) // 2)

    def device(position):
        p = lax.rem(position + 2 * n, n)
        back = p // (n // 2)
        return (1 - back) * (2 * p) + back * (2 * n - 1 - 2 * p)

    return me, place, device


def greet(peers):
    barrier = pltpu.get_barrier_semaphore()
    for peer in peers:
        pl.semaphore_signal(barrier, inc=1, device_id=peer, device_id_type=MESH)
    pl.semaphore_wait(barrier, len(peers))


def ring_peers(axes):
    peers = []
    for axis, n in axes:
        me, place, device = ring_place(axis, n)
        peers += [{axis: device(place + 1)}, {axis: device(place - 1)}]
    return peers


def gather_steps(axes, outs, send_sems, recv_sems):
    rings = [ring_place(axis, n) for axis, n in axes]
    sends = []
    for t in range(max(n for _, n in axes) - 1):
        current = []
        for k, (axis, n) in enumerate(axes):
            if t >= n - 1:
                continue
            me, place, device = rings[k]
            half = outs[k].shape[1] // 2
            for way, sign in enumerate((1, -1)):
                piece = outs[k].at[device(place - sign * t), pl.ds(way * half, half)]
                copy = pltpu.make_async_remote_copy(
                    src_ref=piece,
                    dst_ref=piece,
                    send_sem=send_sems[k].at[way, t],
                    recv_sem=recv_sems[k].at[way, t],
                    device_id={axis: device(place + sign)},
                    device_id_type=MESH,
                )
                copy.start()
                current.append(copy)
        for copy in current:
            copy.wait_recv()
        sends += current
    for copy in sends:
        copy.wait_send()


def gather_kernel(axes, *refs):
    k = len(axes)
    ins, outs, sems = refs[:k], refs[k : 2 * k], refs[2 * k :]
    for (axis, n), own, out in zip(axes, ins, outs):
        out[lax.axis_index(axis)] = own[...]
    greet(ring_peers(axes))
    gather_steps(axes, outs, sems[:k], sems[k:])


def sum_kernel(axes, *refs):
    k = len(axes)
    parts, outs, slots = refs[:k], refs[k : 2 * k], refs[2 * k : 3 * k]
    sems = refs[3 * k :]
    greet(ring_peers(axes))
    rings = [ring_place(axis, n) for axis, n in axes]
    sends = []
    for t in range(max(n for _, n in axes) - 1):
        current = []
        for j, (axis, n) in enumerate(axes):
            if t >= n - 1:
                continue
            me, place, device = rings[j]
            half = parts[j].shape[1] // 2
            for way, sign in enumerate((1, -1)):
                rows = pl.ds(way * half, half)
                piece = device(place - sign * (1 + t))
                if t == 0:
                    source = parts[j].at[piece, rows]
                else:
                    source = slots[j].at[way, t - 1]
                    slots[j][way, t - 1] = slots[j][way, t - 1] + parts[j][piece, rows]
                copy = pltpu.make_async_remote_copy(
                    src_ref=source,
                    dst_ref=slots[j].at[way, t],
                    send_sem=sems[j].at[way, t],
                    recv_sem=sems[k + j].at[way, t],
                    device_id={axis: device(place + sign)},
                    device_id_type=MESH,
                )
                copy.start()
                current.append(copy)
        for copy in current:
            copy.wait_recv()
        sends += current
    for copy in sends:
        copy.wait_send()
    for j, (axis, n) in enumerate(axes):
        me = rings[j][0]
        half = parts[j].shape[1] // 2
        for way in range(2):
            rows = pl.ds(way * half, half)
            outs[j][me, rows] = (slots[j][way, n - 2] + parts[j][me, rows]).astype(outs[j].dtype)
    gather_steps(axes, outs, sems[2 * k : 3 * k], sems[3 * k :])


def dma_sems(axes):
    return [pltpu.SemaphoreType.DMA((2, n - 1)) for _, n in axes]


def vmem_specs(k):
    return [pl.BlockSpec(memory_space=pltpu.VMEM)] * k


def ring_gather(axes, arrays):
    return pl.pallas_call(
        functools.partial(gather_kernel, axes),
        out_shape=[jax.ShapeDtypeStruct((n,) + x.shape, x.dtype) for (_, n), x in zip(axes, arrays)],
        in_specs=vmem_specs(len(axes)),
        out_specs=vmem_specs(len(axes)),
        scratch_shapes=dma_sems(axes) * 2,
        compiler_params=pltpu.CompilerParams(
            collective_id=0, has_side_effects=True, vmem_limit_bytes=40 * 1024 * 1024
        ),
    )(*arrays)


def ring_sum(axes, arrays):
    slots = [pltpu.VMEM((2, n - 1, x.shape[1] // 2, x.shape[2]), x.dtype) for (_, n), x in zip(axes, arrays)]
    return pl.pallas_call(
        functools.partial(sum_kernel, axes),
        out_shape=[jax.ShapeDtypeStruct(x.shape, jnp.bfloat16) for x in arrays],
        in_specs=vmem_specs(len(axes)),
        out_specs=vmem_specs(len(axes)),
        scratch_shapes=slots + dma_sems(axes) * 4,
        compiler_params=pltpu.CompilerParams(
            collective_id=1, has_side_effects=True, vmem_limit_bytes=40 * 1024 * 1024
        ),
    )(*arrays)


def total_kernel(axes, x_ref, out_ref, *refs):
    k = len(axes)
    slots, sems = refs[:k], refs[k:]
    peers = []
    for axis, n in axes:
        me = lax.axis_index(axis)
        peers.append([{axis: lax.rem(me + d, n)} for d in range(1, n)])
    greet(sum(peers, []))
    value = x_ref[...]
    for j, (axis, n) in enumerate(axes):
        me = lax.axis_index(axis)
        slots[j][me] = value
        copies = []
        for d in range(1, n):
            copy = pltpu.make_async_remote_copy(
                src_ref=slots[j].at[me],
                dst_ref=slots[j].at[me],
                send_sem=sems[j].at[d - 1],
                recv_sem=sems[k + j].at[d - 1],
                device_id=peers[j][d - 1],
                device_id_type=MESH,
            )
            copy.start()
            copies.append(copy)
        for copy in copies:
            copy.wait()
        value = slots[j][0]
        for d in range(1, n):
            value = value + slots[j][d]
    out_ref[...] = value


def total_sum(axes, x):
    sems = [pltpu.SemaphoreType.DMA((n - 1,)) for _, n in axes]
    return pl.pallas_call(
        functools.partial(total_kernel, axes),
        out_shape=jax.ShapeDtypeStruct(x.shape, x.dtype),
        in_specs=vmem_specs(1),
        out_specs=pl.BlockSpec(memory_space=pltpu.VMEM),
        scratch_shapes=[pltpu.VMEM((n,) + x.shape, x.dtype) for _, n in axes] + sems * 2,
        compiler_params=pltpu.CompilerParams(collective_id=2, has_side_effects=True),
    )(x)


def local(
    query_grads,
    query_acts,
    train_grads,
    train_acts,
    grad_basis,
    act_basis,
    eigen_corr,
    damping,
    query_seq,
    train_doc,
):
    f32, bf16 = jnp.float32, jnp.bfloat16
    n_row, n_col = lax.axis_size("row"), lax.axis_size("col")
    axes = (("col", n_col), ("row", n_row))
    n_query, n_train = query_seq.shape[0], train_doc.shape[0]
    row_block, col_block = eigen_corr.shape
    own_acts = jnp.concatenate([query_acts, train_acts], axis=0)
    own_grads = jnp.concatenate([query_grads, train_grads], axis=0)
    act_query, grad_query = query_acts.shape[0], query_grads.shape[0]
    pieces = (own_acts.shape[0], own_grads.shape[0], row_block // n_col, (n_query + n_train) // n_row)
    rings = n_row % 2 == 0 and n_col % 2 == 0 and all(size % 32 == 0 for size in pieces)

    def in_order(gathered, first):
        q, t = gathered[:, :first], gathered[:, first:]
        return jnp.concatenate([q.reshape(n_query, -1), t.reshape(n_train, -1)], axis=0)

    if rings:
        acts_all, grads_all = ring_gather(axes, (own_acts, own_grads))
    else:
        acts_all = lax.all_gather(own_acts, "col")
        grads_all = lax.all_gather(own_grads, "row")
    acts_all, grads_all = in_order(acts_all, act_query), in_order(grads_all, grad_query)
    act_part = jnp.dot(acts_all, act_basis, preferred_element_type=f32)
    grad_part = lax.dot_general(
        grad_basis, grads_all, (((0,), (1,)), ((), ())), preferred_element_type=f32
    )
    if rings:
        grads_t, acts_rot = ring_sum(
            axes,
            (
                grad_part.reshape(n_col, row_block // n_col, n_query + n_train),
                act_part.reshape(n_row, (n_query + n_train) // n_row, col_block),
            ),
        )
        grads_t = grads_t.reshape(row_block, n_query + n_train)
        acts_rot = acts_rot.reshape(n_query + n_train, col_block)
    else:
        grads_t = lax.psum(grad_part, "col").astype(bf16)
        acts_rot = lax.psum(act_part, "row").astype(bf16)
    acts_q, acts_ut = acts_rot[:n_query], acts_rot[n_query:].T

    damp = damping.reshape(1, 1)
    seq = query_seq.reshape(n_query, 1)
    partial_scores = block_scores(damp, seq, grads_t, acts_q, acts_ut, eigen_corr) / D

    doc_table = (train_doc[:, None] == jnp.arange(DOCS, dtype=jnp.int32)[None, :]).astype(f32)
    counts = jnp.sum(doc_table, axis=0)
    if rings:
        total = total_sum((("row", n_row), ("col", n_col)), partial_scores)
    else:
        total = lax.psum(partial_scores, ("row", "col"))
    owned = total.shape[1] // n_col
    scores = lax.dynamic_slice_in_dim(total, lax.axis_index("col") * owned, owned, 1)
    doc_sum = jnp.dot(total, doc_table, precision=lax.Precision.HIGHEST)
    return (scores, doc_sum / counts[None, :])


def solution(mesh):
    in_specs = (
        P("row", "col"),
        P("col", "row"),
        P("row", "col"),
        P("col", "row"),
        P("col", "row"),
        P("row", "col"),
        P("row", "col"),
        P(),
        P(),
        P(),
    )
    out_specs = (P(None, "col"), P())
    return jax.shard_map(local, mesh=mesh, in_specs=in_specs, out_specs=out_specs, check_vma=False)
```

time: 830 us -> 330 us (0.40)
  waiting for transfers between devices: 518 us -> 0 us
  Pallas kernels: 123 us -> 298 us
  blocking collectives: 122 us -> 0 us
  between operations: 15 us -> 1.46 us
  matrix products: 23.7 us -> 10.7 us
    reduce_scatter x5 -> x0, waiting for transfers between devices: 281 us -> none  [the longest x4 256 us: local(): lax.psum_scatter(part, 'col', scatter_dimension=0, tiled=True).astype(bf16)]
    pallas_call x4, Pallas kernels: 123 us -> 298 us  [the longest x1 124 us: block_scores(): pl.pallas_call(functools.partial(score_kernel, S, n_query, min(step, 512)...]
    psum x1 -> x0, waiting for transfers between devices: 144 us -> none  [local(): total = lax.psum(partial_scores, ('row', 'col'))]
    all_gather x5 -> x0, blocking collectives: 122 us -> none  [the longest x4 110 us: local(): grads_t = gather(own, 'col')]
    all_gather x4 -> x0, waiting for transfers between devices: 91.3 us -> none  [the longest x1 51 us: local(): gather(train_acts, 'col')]
  transfers between devices with their start and end apart: 10 -> 0, of which waited for: 9 -> 0; matrix products, arithmetic and copies ran while one was open for 4% -> 0% of each run, Pallas kernels for 0% -> 0%
where the time goes in v2:
time: 330 us
  Pallas kernels  298 us (90%)
  local copies, waits for them, and re-layouts  16.5 us (5%)
  matrix products  10.7 us (3%)
    pallas_call x1, Pallas kernels, block_scores(): pl.pallas_call(functools.partial(score_kernel, S, n_query, min(step, 512)...  124 us
    pallas_call x1, Pallas kernels, ring_sum(): pl.pallas_call(functools.partial(sum_kernel, axes), out_shape=[jax.ShapeD...  109 us
    pallas_call x1, Pallas kernels, ring_gather(): pl.pallas_call(functools.partial(gather_kernel, axes), out_shape=[jax.Sha...  37.7 us
    pallas_call x1, Pallas kernels, total_sum(): pl.pallas_call(functools.partial(total_kernel, axes), out_shape=jax.Shape...  26.6 us
    unnamed x17, local copies, waits for them, and re-layouts  6.98 us

profile of v2, /device:TPU:11, one launch (start us, length us, event | category | flops | bytes accessed | tf_op | source)
XLA Modules:
  0.0 330.1 jit_solution(307167774536024929)
XLA Ops:
  0.6 0.0 copy-start.4
  0.6 1.2 pad_maximum_fusion.refs_0_
  1.8 1.2 pad_maximum_fusion.1.refs_1_
  3.0 37.7 %shard_map.113 = (bf16[8,96,2048]{2,1,0:T(8,128)(2,1)S(1)}, bf16[4,192,1024]{2,1,0:T(8,128)(2,1)S(1)}) custom-call(bf16[96,2048]{1,0:T(8,128)(2,1)S(1)} %pad_maximum_fusion.refs_0_, bf16[192,1024]{1,0:T(8,128)(2,1)S(1)} %pad_maximum_fusion.1.refs_1_), custom_call_target="tpu_custom_call" | custom-call | tf_op jit(solution)/shard_map/pallas_call | solution.py:213
  40.8 0.1 slice.19
  40.9 0.0 copy-done.4
  40.9 5.7 %convolution_bitcast_fusion = f32[2048,768]{0,1:T(8,128)} fusion(bf16[1024,2048]{1,0:T(8,128)(2,1)S(1)} %copy-done.4, bf16[512,1024]{1,0:T(8,128)(2,1)S(1)} %bitcast.26, bf16[256,1024]{1,0:T(8,128)(2,1)S(1)} %bitcast.28), kind=kOutput, calls=%fused_computation | convolution fusion | flops 3224371200 | bytes 12058624 | tf_op jit(solution)/shard_map/dot_general | solution.py:317
  46.6 6.6 %copy.18 = f32[2048,768]{1,0:T(8,128)} copy(f32[2048,768]{0,1:T(8,128)} %convolution_bitcast_fusion) | data formatting | bytes 12582912 | tf_op jit(solution)/shard_map/dot_general | solution.py:317
  53.2 0.0 copy-start.5
  53.2 0.1 slice.21
  53.3 0.0 slice-start
  53.3 0.1 slice.20
  53.4 2.0 copy-done.5
  55.4 3.4 %fusion = f32[768,1024]{1,0:T(8,128)S(1)} fusion(bf16[2048,1024]{1,0:T(8,128)(2,1)S(1)} %copy-done.5, bf16[512,2048]{1,0:T(8,128)(2,1)S(1)} %bitcast.25, bf16[256,2048]{1,0:T(8,128)(2,1)S(1)} %bitcast.27), kind=kOutput, calls=%fused_computation.1 | convolution fusion | flops 3227516928 | bytes 10485760 | tf_op jit(solution)/shard_map/dot_general | solution.py:316
  58.8 0.0 slice-done
  58.8 0.0 slice-done.1
  58.8 109.5 %shard_map.114 = (bf16[8,256,768]{2,1,0:T(8,128)(2,1)S(1)}, bf16[4,192,1024]{2,1,0:T(8,128)(2,1)S(1)}) custom-call(f32[8,256,768]{2,1,0:T(8,128)S(1)} %bitcast.19, f32[4,192,1024]{2,1,0:T(8,128)S(1)} %bitcast.20), custom_call_target="tpu_custom_call" | custom-call | tf_op jit(solution)/shard_map/pallas_call | solution.py:227
  168.3 0.0 copy-start
  168.3 1.6 copy-done
  169.9 1.1 slice.25
  171.0 1.5 copy.21
  172.5 0.0 copy-done.3
  172.5 0.1 copy.20.seq_ref
  173.3 0.0 copy-start.1
  173.3 1.9 copy-done.1
  175.2 124.5 %shard_map.115 = f32[32,512]{1,0:T(8,128)S(1)} custom-call(f32[1,1]{1,0:T(1,128)} %bitcast.16.damp_ref, s32[256,1]{1,0:T(8,128)S(1)} %copy.20.seq_ref, bf16[2048,768]{1,0:T(8,128)(2,1)S(1)} %bitcast.24, bf16[256,1024]{1,0:T(8,128)(2,1)S(1)} %slice.24.aq_ref, bf16[1024,512]{1,0:T(8,128)(2,1)S(1)} %bitcast.23, f32[2048,1024]{1,0:T(8,128)} %eig_ref.1), custom_call_target="tpu_custom_call" | custom-call | flops 103079215104 | bytes 8388608 | tf_op jit(solution)/shard_map/pallas_call | solution.py:63
  299.7 0.6 broadcast_multiply_fusion.x_ref
  300.4 26.6 %shard_map.116 = f32[32,512]{1,0:T(8,128)} custom-call(f32[32,512]{1,0:T(8,128)} %broadcast_multiply_fusion.x_ref), custom_call_target="tpu_custom_call" | custom-call | tf_op jit(solution)/shard_map/pallas_call | solution.py:273
  327.0 1.4 constant_dynamic-slice_fusion
  328.4 0.0 copy-done.2
  328.4 0.1 convert_reduce_fusion
  328.5 1.6 convolution_divide_fusion
  (6 shorter events, 0.1 us)
Async XLA Ops:
  0.6 40.3 %copy-start.4 = (bf16[1024,2048]{1,0:T(8,128)(2,1)S(1)}, bf16[1024,2048]{1,0:T(8,128)(2,1)}, u32[]{:S(2)}) copy-start(bf16[1024,2048]{1,0:T(8,128)(2,1)} %param.14) | copy-start | bytes 12582916
  53.2 2.2 copy-start.5
  53.3 5.5 %slice-start = ((s8[6291456]{0:T(1024)(128)(4,1)}), s8[4194304]{0:T(1024)(128)(4,1)S(1)}, s32[]{:S(2)}) async-start(s8[6291456]{0:T(1024)(128)(4,1)} %bitcast.17), calls=%async_computation | async-start | bytes 8388608
  55.4 3.4 %slice-start.1 = ((s8[6291456]{0:T(1024)(128)(4,1)}), s8[2097152]{0:T(1024)(128)(4,1)S(1)}, s32[]{:S(2)}) async-start(s8[6291456]{0:T(1024)(128)(4,1)} %bitcast.17), calls=%async_computation.1 | async-start | bytes 4194304
  168.3 1.6 copy-start
  169.9 2.6 copy-start.3
  173.3 1.9 copy-start.1
  175.2 153.1 %copy-start.2 = (s32[512]{0:T(512)S(1)}, s32[512]{0:T(512)}, u32[]{:S(2)}) copy-start(s32[512]{0:T(512)} %param.19) | copy-start | bytes 6148

commit v3 on v2

--- a/solution.py
+++ b/solution.py
@@ -172,11 +172,12 @@
             for way, sign in enumerate((1, -1)):
                 rows = pl.ds(way * half, half)
                 piece = device(place - sign * (1 + t))
-                if t == 0:
-                    source = parts[j].at[piece, rows]
-                else:
-                    source = slots[j].at[way, t - 1]
-                    slots[j][way, t - 1] = slots[j][way, t - 1] + parts[j][piece, rows]
+                running = parts[j][piece, rows]
+                if t > 0:
+                    running = running + slots[j][way, t - 1].astype(jnp.float32)
+                here = (t - 1) % n
+                slots[j][way, here] = running.astype(slots[j].dtype)
+                source = slots[j].at[way, here]
                 copy = pltpu.make_async_remote_copy(
                     src_ref=source,
                     dst_ref=slots[j].at[way, t],
@@ -197,7 +198,8 @@
         half = parts[j].shape[1] // 2
         for way in range(2):
             rows = pl.ds(way * half, half)
-            outs[j][me, rows] = (slots[j][way, n - 2] + parts[j][me, rows]).astype(outs[j].dtype)
+            last = slots[j][way, n - 2].astype(jnp.float32)
+            outs[j][me, rows] = (last + parts[j][me, rows]).astype(outs[j].dtype)
     gather_steps(axes, outs, sems[2 * k : 3 * k], sems[3 * k :])
 
 
@@ -222,8 +224,11 @@
     )(*arrays)
 
 
-def ring_sum(axes, arrays):
-    slots = [pltpu.VMEM((2, n - 1, x.shape[1] // 2, x.shape[2]), x.dtype) for (_, n), x in zip(axes, arrays)]
+def ring_sum(axes, arrays, wires):
+    slots = [
+        pltpu.VMEM((2, n, x.shape[1] // 2, x.shape[2]), wire)
+        for (_, n), x, wire in zip(axes, arrays, wires)
+    ]
     return pl.pallas_call(
         functools.partial(sum_kernel, axes),
         out_shape=[jax.ShapeDtypeStruct(x.shape, jnp.bfloat16) for x in arrays],
@@ -324,6 +329,7 @@
                 grad_part.reshape(n_col, row_block // n_col, n_query + n_train),
                 act_part.reshape(n_row, (n_query + n_train) // n_row, col_block),
             ),
+            (bf16, f32),
         )
         grads_t = grads_t.reshape(row_block, n_query + n_train)
         acts_rot = acts_rot.reshape(n_query + n_train, col_block)

time: 330 us -> 318 us (0.964)
  Pallas kernels: 298 us -> 286 us
    pallas_call x1, Pallas kernels: 109 us -> 97 us  [ring_sum(): pl.pallas_call(functools.partial(sum_kernel, axes), out_shape=[jax.ShapeD...]
where the time goes in v3:
time: 318 us
  Pallas kernels  286 us (90%)
  local copies, waits for them, and re-layouts  16.5 us (5%)
  matrix products  10.7 us (3%)
    pallas_call x1, Pallas kernels, block_scores(): pl.pallas_call(functools.partial(score_kernel, S, n_query, min(step, 512)...  124 us
    pallas_call x1, Pallas kernels, ring_sum(): pl.pallas_call(functools.partial(sum_kernel, axes), out_shape=[jax.ShapeD...  97 us
    pallas_call x1, Pallas kernels, ring_gather(): pl.pallas_call(functools.partial(gather_kernel, axes), out_shape=[jax.Sha...  37.7 us
    pallas_call x1, Pallas kernels, total_sum(): pl.pallas_call(functools.partial(total_kernel, axes), out_shape=jax.Shape...  26.8 us
    unnamed x17, local copies, waits for them, and re-layouts  6.98 us
    dot_general x1, local copies, waits for them, and re-layouts, local(): lax.dot_general(grad_basis, grads_all, (((0,), (1,)), ((), ())), preferre...  6.56 us

profile of v3, /device:TPU:11, one launch (start us, length us, event | category | flops | bytes accessed | tf_op | source)
XLA Modules:
  0.0 317.8 jit_solution(18049923995199086630)
XLA Ops:
  0.6 0.0 copy-start.4
  0.6 1.2 pad_maximum_fusion.refs_0_
  1.8 1.2 pad_maximum_fusion.1.refs_1_
  3.0 37.7 %shard_map.113 = (bf16[8,96,2048]{2,1,0:T(8,128)(2,1)S(1)}, bf16[4,192,1024]{2,1,0:T(8,128)(2,1)S(1)}) custom-call(bf16[96,2048]{1,0:T(8,128)(2,1)S(1)} %pad_maximum_fusion.refs_0_, bf16[192,1024]{1,0:T(8,128)(2,1)S(1)} %pad_maximum_fusion.1.refs_1_), custom_call_target="tpu_custom_call" | custom-call | tf_op jit(solution)/shard_map/pallas_call | solution.py:215
  40.8 0.1 slice.19
  40.9 0.0 copy-done.4
  40.9 5.7 %convolution_bitcast_fusion = f32[2048,768]{0,1:T(8,128)} fusion(bf16[1024,2048]{1,0:T(8,128)(2,1)S(1)} %copy-done.4, bf16[512,1024]{1,0:T(8,128)(2,1)S(1)} %bitcast.26, bf16[256,1024]{1,0:T(8,128)(2,1)S(1)} %bitcast.28), kind=kOutput, calls=%fused_computation | convolution fusion | flops 3224371200 | bytes 12058624 | tf_op jit(solution)/shard_map/dot_general | solution.py:322
  46.6 6.6 %copy.18 = f32[2048,768]{1,0:T(8,128)} copy(f32[2048,768]{0,1:T(8,128)} %convolution_bitcast_fusion) | data formatting | bytes 12582912 | tf_op jit(solution)/shard_map/dot_general | solution.py:322
  53.2 0.0 copy-start.5
  53.2 0.1 slice.21
  53.3 0.0 slice-start
  53.3 0.1 slice.20
  53.4 2.0 copy-done.5
  55.4 3.4 %fusion = f32[768,1024]{1,0:T(8,128)S(1)} fusion(bf16[2048,1024]{1,0:T(8,128)(2,1)S(1)} %copy-done.5, bf16[512,2048]{1,0:T(8,128)(2,1)S(1)} %bitcast.25, bf16[256,2048]{1,0:T(8,128)(2,1)S(1)} %bitcast.27), kind=kOutput, calls=%fused_computation.1 | convolution fusion | flops 3227516928 | bytes 10485760 | tf_op jit(solution)/shard_map/dot_general | solution.py:321
  58.8 0.0 slice-done
  58.8 0.0 slice-done.1
  58.8 97.0 %shard_map.114 = (bf16[8,256,768]{2,1,0:T(8,128)(2,1)S(1)}, bf16[4,192,1024]{2,1,0:T(8,128)(2,1)S(1)}) custom-call(f32[8,256,768]{2,1,0:T(8,128)S(1)} %bitcast.19, f32[4,192,1024]{2,1,0:T(8,128)S(1)} %bitcast.20), custom_call_target="tpu_custom_call" | custom-call | tf_op jit(solution)/shard_map/pallas_call | solution.py:232
  155.8 0.0 copy-start
  155.8 1.6 copy-done
  157.4 1.1 slice.25
  158.5 1.5 copy.21
  160.0 0.0 copy-done.3
  160.0 0.1 copy.20.seq_ref
  160.8 0.0 copy-start.1
  160.8 1.9 copy-done.1
  162.7 124.5 %shard_map.115 = f32[32,512]{1,0:T(8,128)S(1)} custom-call(f32[1,1]{1,0:T(1,128)} %bitcast.16.damp_ref, s32[256,1]{1,0:T(8,128)S(1)} %copy.20.seq_ref, bf16[2048,768]{1,0:T(8,128)(2,1)S(1)} %bitcast.24, bf16[256,1024]{1,0:T(8,128)(2,1)S(1)} %slice.24.aq_ref, bf16[1024,512]{1,0:T(8,128)(2,1)S(1)} %bitcast.23, f32[2048,1024]{1,0:T(8,128)} %eig_ref.1), custom_call_target="tpu_custom_call" | custom-call | flops 103079215104 | bytes 8388608 | tf_op jit(solution)/shard_map/pallas_call | solution.py:63
  287.2 0.6 broadcast_multiply_fusion.x_ref
  287.8 26.8 %shard_map.116 = f32[32,512]{1,0:T(8,128)} custom-call(f32[32,512]{1,0:T(8,128)} %broadcast_multiply_fusion.x_ref), custom_call_target="tpu_custom_call" | custom-call | tf_op jit(solution)/shard_map/pallas_call | solution.py:278
  314.6 1.4 constant_dynamic-slice_fusion
  316.0 0.0 copy-done.2
  316.0 0.1 convert_reduce_fusion
  316.2 1.6 convolution_divide_fusion
  (6 shorter events, 0.1 us)
Async XLA Ops:
  0.6 40.3 %copy-start.4 = (bf16[1024,2048]{1,0:T(8,128)(2,1)S(1)}, bf16[1024,2048]{1,0:T(8,128)(2,1)}, u32[]{:S(2)}) copy-start(bf16[1024,2048]{1,0:T(8,128)(2,1)} %param.14) | copy-start | bytes 12582916
  53.2 2.2 copy-start.5
  53.3 5.5 %slice-start = ((s8[6291456]{0:T(1024)(128)(4,1)}), s8[4194304]{0:T(1024)(128)(4,1)S(1)}, s32[]{:S(2)}) async-start(s8[6291456]{0:T(1024)(128)(4,1)} %bitcast.17), calls=%async_computation | async-start | bytes 8388608
  55.4 3.4 %slice-start.1 = ((s8[6291456]{0:T(1024)(128)(4,1)}), s8[2097152]{0:T(1024)(128)(4,1)S(1)}, s32[]{:S(2)}) async-start(s8[6291456]{0:T(1024)(128)(4,1)} %bitcast.17), calls=%async_computation.1 | async-start | bytes 4194304
  155.8 1.6 copy-start
  157.4 2.6 copy-start.3
  160.8 1.9 copy-start.1
  162.7 153.3 %copy-start.2 = (s32[512]{0:T(512)S(1)}, s32[512]{0:T(512)}, u32[]{:S(2)}) copy-start(s32[512]{0:T(512)} %param.19) | copy-start | bytes 6148
